TPU v7x, 32 devices: a whole 2x2x4 slice. The times are simulated.
32 devices in a mesh: groups: 2 (over y), mp: 8 (over z, x), dp: 2 (over core).
Axes of the slice: x: 2, y: 2, z: 4, core: 2. Of those that a mesh axis runs over, the one named last changes fastest.
Arguments:
- queries: bfloat16 [4, 1024, 2048], P(('groups', 'dp'), 'mp'), parts along dimension 0
- keys: bfloat16 [4, 1024, 2048], P(('groups', 'dp'), 'mp'), parts along dimension 0
- values: bfloat16 [4, 1024, 2048], P(('groups', 'dp'), 'mp'), parts along dimension 0, may hold values from -6 to 6
- grad_out: bfloat16 [4, 1024, 2048], P(('groups', 'dp'), 'mp'), parts along dimension 0, may hold values from -6 to 6
- neighbours: int32 [4, 8, 4], P(('groups', 'dp'), 'mp'), parts along dimension 0, may hold values from -1 to 7, as said below
- counts: int32 [4, 8], P(('groups', 'dp'), 'mp'), parts along dimension 0, may hold values from 1 to 4, as said below
Outputs:
- attended: bfloat16 [4, 1024, 2048], P(('groups', 'dp'), 'mp'), parts along dimension 0
- grad_queries: bfloat16 [4, 1024, 2048], P(('groups', 'dp'), 'mp'), parts along dimension 0
- grad_keys: bfloat16 [4, 1024, 2048], P(('groups', 'dp'), 'mp'), parts along dimension 0
- grad_values: bfloat16 [4, 1024, 2048], P(('groups', 'dp'), 'mp'), parts along dimension 0
There are 2 independent parts, one for each index of `groups`. A program takes and returns all parts, laid end to end along the dimension named above; each array names one. Nothing has to cross between parts.
Inputs may be any that keep to these rules, and one draw needn't show every extreme that they name: The first counts[b, t] entries of neighbours[b, t, :] are distinct tiles t + o of the same row with 1 <= |o| <= 2; the other entries are -1. `counts`: every row has a tile with 4 listed tiles and a tile with one.
All inputs are finite; a program needn't handle non-finite values.
Results may differ from a plain program's by a relative error of at most 0.0085.
Values may be sent and summed in bfloat16 or wider, within the bound.
A program may use at most 64 MiB of HBM per device.

v0:
```python
import jax
import jax.numpy as jnp
from jax import lax
from jax.sharding import PartitionSpec as P

HEADS = 16
HEAD_DIM = 128
TILE = 128
REACH = 2
MAXN = 4


def passed_along(array, axis, by):
    peers = lax.axis_size(axis)
    pairs = [(i, i + by) for i in range(peers) if 0 <= i + by < peers]
    return lax.ppermute(array, axis, pairs)


def window_present(neighbours, counts):
    position = lax.axis_index("mp")
    listed = neighbours[:, 0, :]
    listed_count = counts[:, 0]
    places = jnp.arange(MAXN, dtype=jnp.int32)
    columns = []
    for offset in range(-REACH, REACH + 1):
        if offset == 0:
            columns.append(jnp.ones(listed_count.shape, jnp.bool_))
        else:
            hits = (listed == position + offset) & (places[None, :] < listed_count[:, None])
            columns.append(jnp.any(hits, axis=1))
    return jnp.stack(columns, axis=1)


def direct_window(key_value):
    pieces = []
    for offset in range(-REACH, REACH + 1):
        if offset == 0:
            pieces.append(key_value)
        else:
            pieces.append(passed_along(key_value, "mp", -offset))
    return jnp.concatenate(pieces, axis=2)


def local(queries, keys, values, grad_out, neighbours, counts):
    window_size = 2 * REACH + 1
    inv_root = HEAD_DIM ** (-0.5)
    rows_here = queries.shape[0]
    features = queries.shape[2]
    present = window_present(neighbours, counts)
    key_value = jnp.stack([keys, values])
    window = direct_window(key_value)
    key_heads = window[0].reshape(rows_here, window_size * TILE, HEADS, HEAD_DIM)
    value_heads = window[1].reshape(rows_here, window_size * TILE, HEADS, HEAD_DIM)
    query_heads = queries.reshape(rows_here, TILE, HEADS, HEAD_DIM)
    grad_heads = grad_out.reshape(rows_here, TILE, HEADS, HEAD_DIM)
    scores = (
        jnp.einsum("bqhe,bkhe->bhqk", query_heads, key_heads, preferred_element_type=jnp.float32)
        * inv_root
    )
    keymask = jnp.repeat(present, TILE, axis=1)
    scores = jnp.where(keymask[:, None, None, :], scores, -jnp.inf)
    row_max = jnp.max(scores, axis=-1, keepdims=True)
    exponent = jnp.exp(scores - row_max)
    row_sum = jnp.sum(exponent, axis=-1, keepdims=True)
    weights = exponent / row_sum
    weights_low = weights.astype(jnp.bfloat16)
    mixture = jnp.einsum(
        "bhqk,bkhe->bqhe", weights_low, value_heads, preferred_element_type=jnp.float32
    )
    attended = mixture.reshape(rows_here, TILE, features).astype(jnp.bfloat16)
    grad_prob = jnp.einsum(
        "bqhe,bkhe->bhqk", grad_heads, value_heads, preferred_element_type=jnp.float32
    )
    row_delta = jnp.transpose(
        jnp.sum(grad_heads.astype(jnp.float32) * mixture, axis=-1), (0, 2, 1)
    )[..., None]
    dscore = (weights * (grad_prob - row_delta) * inv_root).astype(jnp.bfloat16)
    grad_queries = jnp.einsum(
        "bhqk,bkhe->bqhe", dscore, key_heads, preferred_element_type=jnp.float32
    )
    grad_queries = grad_queries.reshape(rows_here, TILE, features).astype(jnp.bfloat16)
    own_begin = REACH * TILE
    own_keys = keys.reshape(rows_here, TILE, HEADS, HEAD_DIM)
    own_values = values.reshape(rows_here, TILE, HEADS, HEAD_DIM)
    own_dscore = dscore[..., own_begin : own_begin + TILE]
    own_low = weights_low[..., own_begin : own_begin + TILE]
    key_sum = jnp.einsum(
        "bhqk,bqhe->bkhe", own_dscore, query_heads, preferred_element_type=jnp.float32
    )
    key_sum = key_sum.reshape(rows_here, TILE, features).astype(jnp.bfloat16).astype(jnp.float32)
    value_sum = jnp.einsum(
        "bhqk,bqhe->bkhe", own_low, grad_heads, preferred_element_type=jnp.float32
    )
    value_sum = (
        value_sum.reshape(rows_here, TILE, features).astype(jnp.bfloat16).astype(jnp.float32)
    )
    outgoing = jnp.stack([queries, grad_out])
    for slot, offset in enumerate(range(-REACH, REACH + 1)):
        if offset == 0:
            continue
        uses_me = present[:, slot].astype(jnp.int32)
        incoming = passed_along(outgoing, "mp", offset)
        far_max, far_sum, far_delta, far_uses = passed_along(
            (row_max, row_sum, row_delta, uses_me), "mp", offset
        )
        active = (far_uses > 0)[:, None, None, None]
        far_query = incoming[0].reshape(rows_here, TILE, HEADS, HEAD_DIM)
        far_grad = incoming[1].reshape(rows_here, TILE, HEADS, HEAD_DIM)
        far_scores = (
            jnp.einsum("bqhe,bkhe->bhqk", far_query, own_keys, preferred_element_type=jnp.float32)
            * inv_root
        )
        safe_sum = jnp.where(active, far_sum, 1.0)
        far_weights = jnp.where(active, jnp.exp(far_scores - far_max) / safe_sum, 0.0)
        far_low = far_weights.astype(jnp.bfloat16)
        far_prob = jnp.einsum(
            "bqhe,bkhe->bhqk", far_grad, own_values, preferred_element_type=jnp.float32
        )
        far_dscore = (far_weights * (far_prob - far_delta) * inv_root).astype(jnp.bfloat16)
        far_key = jnp.einsum(
            "bhqk,bqhe->bkhe", far_dscore, far_query, preferred_element_type=jnp.float32
        )
        key_sum = key_sum + far_key.reshape(rows_here, TILE, features).astype(jnp.bfloat16).astype(
            jnp.float32
        )
        far_value = jnp.einsum(
            "bhqk,bqhe->bkhe", far_low, far_grad, preferred_element_type=jnp.float32
        )
        value_sum = value_sum + far_value.reshape(rows_here, TILE, features).astype(
            jnp.bfloat16
        ).astype(jnp.float32)
    grad_keys = key_sum.astype(jnp.bfloat16)
    grad_values = value_sum.astype(jnp.bfloat16)
    return (attended, grad_queries, grad_keys, grad_values)


def solution(mesh):
    return jax.shard_map(
        local,
        mesh=mesh,
        in_specs=(
            P(("groups", "dp"), "mp", None),
            P(("groups", "dp"), "mp", None),
            P(("groups", "dp"), "mp", None),
            P(("groups", "dp"), "mp", None),
            P(("groups", "dp"), "mp", None),
            P(("groups", "dp"), "mp"),
        ),
        out_specs=(
            P(("groups", "dp"), "mp", None),
            P(("groups", "dp"), "mp", None),
            P(("groups", "dp"), "mp", None),
            P(("groups", "dp"), "mp", None),
        ),
        check_vma=False,
    )
```

profile of v0, /device:TPU:30, one launch (start us, length us, event | category | flops | bytes accessed | tf_op | source)
XLA Modules:
  0.0 203.7 jit_solution(7708644378617689153)
XLA Ops:
  0.7 1.4 copy.39
  2.1 1.3 copy.38
  3.4 1.1 pad_maximum_fusion
  4.5 1.3 collective-permute-start
  5.7 1.3 collective-permute-start.1
  7.0 5.6 %collective-permute-start.2 = (bf16[2,1,128,2048]{2,3,1,0:T(8,128)(2,1)}, bf16[2,1,128,2048]{2,3,1,0:T(8,128)(2,1)}, u32[]{:S(2)}, u32[]{:S(2)}) collective-permute-start(bf16[2,1,128,2048]{2,3,1,0:T(8,128)(2,1)} %pad_maximum_fusion), channel_id=1, source_target_pairs={{2,0},{4,2},{6,4},{8,6},{10,8},{12,10},{14,12},{3,1},{5,3},{7,5},{... | collective-permute-start | bytes 3145736 | tf_op jit(solution)/shard_map/ppermute | solution.py:16
  12.6 4.5 %collective-permute-start.3 = (bf16[2,1,128,2048]{2,3,1,0:T(8,128)(2,1)}, bf16[2,1,128,2048]{2,3,1,0:T(8,128)(2,1)}, u32[]{:S(2)}, u32[]{:S(2)}) collective-permute-start(bf16[2,1,128,2048]{2,3,1,0:T(8,128)(2,1)} %pad_maximum_fusion), channel_id=1, source_target_pairs={{4,0},{6,2},{8,4},{10,6},{12,8},{14,10},{5,1},{7,3},{9,5},{11,7},{... | collective-permute-start | bytes 3145736 | tf_op jit(solution)/shard_map/ppermute | solution.py:16
  17.8 1.4 fusion.84
  19.8 1.3 collective-permute-start.20
  21.1 1.3 copy.77
  22.7 1.1 pad_maximum_fusion.1
  23.8 2.7 %stack.42 = pred[1,5]{1,0:T(4,128)(4,1)S(1)} concatenate(pred[1,1]{1,0:T(4,128)(4,1)} %bitcast.5, pred[1,1]{1,0:T(4,128)(4,1)} %bitcast.7, pred[1,1]{1,0:T(4,128)(4,1)} %constant.6.clone.1, pred[1,1]{1,0:T(4,128)(4,1)} %bitcast.9, pred[1,1]{1,0:T(4,128)(4,1)} %bitcast.11), dimensions={1} | concatenate | bytes 10 | tf_op jit(solution)/shard_map/stack | solution.py:31
  26.5 1.2 copy.45
  29.7 0.9 copy.79
  30.6 23.3 %collective-permute-done.20 = s32[1]{0:T(128)} collective-permute-done((s32[1]{0:T(128)}, s32[1]{0:T(128)}, u32[]{:S(2)}, u32[]{:S(2)}) %collective-permute-start.20) | collective-permute-done | bytes 36 | tf_op jit(solution)/shard_map/ppermute | solution.py:16
  53.9 1.3 collective-permute-start.15
  55.9 3.6 %collective-permute-done.15 = s32[1]{0:T(128)} collective-permute-done((s32[1]{0:T(128)}, s32[1]{0:T(128)}, u32[]{:S(2)}, u32[]{:S(2)}) %collective-permute-start.15) | collective-permute-done | bytes 36 | tf_op jit(solution)/shard_map/ppermute | solution.py:16
  59.4 11.8 %collective-permute-start.10 = (s32[1]{0:T(128)}, s32[1]{0:T(128)}, u32[]{:S(2)}, u32[]{:S(2)}) collective-permute-start(s32[1]{0:T(128)} %bitcast.46), channel_id=1, source_target_pairs={{2,0},{4,2},{6,4},{8,6},{10,8},{12,10},{14,12},{3,1},{5,3},{7,5},{... | collective-permute-start | bytes 20 | tf_op jit(solution)/shard_map/ppermute | solution.py:16
  71.9 6.2 %collective-permute-start.5 = (s32[1]{0:T(128)}, s32[1]{0:T(128)}, u32[]{:S(2)}, u32[]{:S(2)}) collective-permute-start(s32[1]{0:T(128)} %bitcast.34), channel_id=1, source_target_pairs={{4,0},{6,2},{8,4},{10,6},{12,8},{14,10},{5,1},{7,3},{9,5},{11,7},{... | collective-permute-start | bytes 20 | tf_op jit(solution)/shard_map/ppermute | solution.py:16
  78.8 1.3 collective-permute-start.19
  80.6 1.3 collective-permute-start.14
  81.9 1.4 constant_dynamic-update-slice_fusion.4
  83.3 4.6 %collective-permute-start.9 = (bf16[2,1,128,2048]{2,3,1,0:T(8,128)(2,1)}, bf16[2,1,128,2048]{2,3,1,0:T(8,128)(2,1)S(1)}, u32[]{:S(2)}, u32[]{:S(2)}) collective-permute-start(bf16[2,1,128,2048]{2,3,1,0:T(8,128)(2,1)} %pad_maximum_fusion.1), channel_id=1, source_target_pairs={{2,0},{4,2},{6,4},{8,6},{10,8},{12,10},{14,12},{3,1},{5,3},{7,5},{... | collective-permute-start | bytes 3145736 | tf_op jit(solution)/shard_map/ppermute | solution.py:16
  88.0 1.5 constant_dynamic-update-slice_fusion.3
  89.7 4.5 %collective-permute-start.4 = (bf16[2,1,128,2048]{2,3,1,0:T(8,128)(2,1)S(1)}, bf16[2,1,128,2048]{2,3,1,0:T(8,128)(2,1)S(1)}, u32[]{:S(2)}, u32[]{:S(2)}) collective-permute-start(bf16[2,1,128,2048]{2,3,1,0:T(8,128)(2,1)S(1)} %copy-done.7), channel_id=1, source_target_pairs={{4,0},{6,2},{8,4},{10,6},{12,8},{14,10},{5,1},{7,3},{9,5},{11,7},{... | collective-permute-start | bytes 3145736 | tf_op jit(solution)/shard_map/ppermute | solution.py:16
  94.3 1.5 constant_dynamic-update-slice_fusion.1
  95.8 1.5 constant_dynamic-update-slice_fusion
  97.7 1.4 bitcast_reduce_fusion
  99.2 1.1 fusion.4
  100.3 2.8 %multiply_reduce_fusion = (f32[128,16]{0,1:T(8,128)S(1)}, bf16[1,128,16,128]{1,3,2,0:T(8,128)(2,1)}) fusion(f32[1,128,16,128]{1,3,2,0:T(8,128)S(1)} %bitcast.204, bf16[640,16,128]{0,2,1:T(8,128)(2,1)S(1)} %bitcast.190, f32[16,128]{1,0:T(8,128)S(1)} %fusion.4, f32[16,128]{1,0:T(8,128)S(1)} %get-tuple-element.28, f32[16,640,128]{2,1,0:T(8,128)S(1)} %get-tuple-element.29, ...), kind=kOutput, calls=%fused_computation.79 | convolution fusion | flops 342882304 | bytes 9462400 | tf_op jit(solution)/shard_map/bhqk,bkhe->bqhe/dot_general | solution.py:67
  103.1 2.7 %fusion.1 = bf16[16,128,640]{1,2,0:T(8,128)(2,1)S(1)} fusion(f32[16,128]{1,0:T(8,128)S(1)} %bitcast.223, bf16[640,16,128]{0,2,1:T(8,128)(2,1)S(1)} %bitcast.191, bf16[128,16,128]{0,2,1:T(8,128)(2,1)S(1)} %bitcast.179, f32[16,128]{1,0:T(8,128)S(1)} %fusion.4, f32[16,128]{1,0:T(8,128)S(1)} %get-tuple-element.28, f32[16,640,128]{2,1,0:T(8,128)S(1)} %get-tuple-element.29, ...), kind=kOutput, calls=%fused_computation.2 | convolution fusion | flops 346030080 | bytes 11035264 | tf_op jit(solution)/shard_map/bqhe,bkhe->bhqk/dot_general | solution.py:71
  105.8 1.6 convolution_convert_fusion.10
  107.4 1.3 collective-permute-start.22
  108.7 1.3 collective-permute-start.17
  110.9 1.3 collective-permute-start.21
  113.1 15.9 %collective-permute-done.9 = bf16[2,1,128,2048]{2,3,1,0:T(8,128)(2,1)S(1)} collective-permute-done((bf16[2,1,128,2048]{2,3,1,0:T(8,128)(2,1)}, bf16[2,1,128,2048]{2,3,1,0:T(8,128)(2,1)S(1)}, u32[]{:S(2)}, u32[]{:S(2)}) %collective-permute-start.9) | collective-permute-done | bytes 1048608 | tf_op jit(solution)/shard_map/ppermute | solution.py:16
  129.0 1.5 collective-permute-start.16
  131.3 1.5 fusion.27
  132.8 1.6 convert_bitcast_fusion
  135.3 1.5 fusion.38
  136.8 2.0 %copy.61 = bf16[1,128,2048]{2,1,0:T(8,128)(2,1)} copy(bf16[1,128,2048]{1,2,0:T(8,128)(2,1)} %bitcast.209) | data formatting | bytes 1048576
  138.8 2.0 %copy.62 = bf16[1,128,2048]{2,1,0:T(8,128)(2,1)} copy(bf16[1,128,2048]{1,2,0:T(8,128)(2,1)} %bitcast.203) | data formatting | bytes 1048576
  140.9 1.3 collective-permute-start.23
  142.2 1.3 collective-permute-start.18
  143.5 5.6 %collective-permute-start.12 = (f32[1,16,128,1]{2,1,3,0:T(8,128)S(1)}, f32[1,16,128,1]{2,1,3,0:T(8,128)S(1)}, u32[]{:S(2)}, u32[]{:S(2)}) collective-permute-start(f32[1,16,128,1]{2,1,3,0:T(8,128)S(1)} %bitcast.216), channel_id=1, source_target_pairs={{2,0},{4,2},{6,4},{8,6},{10,8},{12,10},{14,12},{3,1},{5,3},{7,5},{... | collective-permute-start | bytes 24584 | tf_op jit(solution)/shard_map/ppermute | solution.py:16
  149.1 3.1 %fusion.9 = f32[16,128,128]{2,1,0:T(8,128)} fusion(bf16[128,16,128]{0,2,1:T(8,128)(2,1)} %bitcast.201, f32[16,128]{1,0:T(8,128)S(1)} %select_bitcast_fusion, f32[16,128]{1,0:T(8,128)S(1)} %bitcast.229, bf16[128,16,128]{2,1,0:T(8,128)(2,1)} %bitcast.205), kind=kOutput, calls=%fused_computation.15 | convolution fusion | flops 67895296 | bytes 2113536 | tf_op jit(solution)/shard_map/bqhe,bkhe->bhqk/dot_general | solution.py:110
  152.2 5.5 %collective-permute-start.11 = (f32[1,16,128,1]{2,1,3,0:T(8,128)S(1)}, f32[1,16,128,1]{2,1,3,0:T(8,128)S(1)}, u32[]{:S(2)}, u32[]{:S(2)}) collective-permute-start(f32[1,16,128,1]{2,1,3,0:T(8,128)S(1)} %bitcast.212), channel_id=1, source_target_pairs={{2,0},{4,2},{6,4},{8,6},{10,8},{12,10},{14,12},{3,1},{5,3},{7,5},{... | collective-permute-start | bytes 24584 | tf_op jit(solution)/shard_map/ppermute | solution.py:16
  157.6 3.1 %fusion.36 = f32[16,128,128]{2,1,0:T(8,128)} fusion(bf16[128,16,128]{0,2,1:T(8,128)(2,1)} %bitcast.202, bf16[128,16,128]{0,2,1:T(8,128)(2,1)S(1)} %bitcast.187, bf16[128,16,128]{0,2,1:T(8,128)(2,1)S(1)} %bitcast.167, f32[16,128,128]{2,1,0:T(8,128)} %fusion.9, f32[16,128]{1,0:T(8,128)S(1)} %bitcast.221, pred[]{:T(512)} %bitcast.62), kind=kOutput, calls=%fused_computation.61 | convolution fusion | flops 136052736 | bytes 3678209 | tf_op jit(solution)/shard_map/bhqk,bqhe->bkhe/dot_general | solution.py:120
  160.7 2.5 %fusion.47 = f32[16,128,128]{2,1,0:T(8,128)} fusion(bf16[128,16,128]{0,2,1:T(8,128)(2,1)S(1)} %bitcast.188, f32[16,128,128]{2,1,0:T(8,128)} %fusion.9, pred[]{:T(512)} %bitcast.62), kind=kOutput, calls=%fused_computation.72 | convolution fusion | flops 67895296 | bytes 2621441 | tf_op jit(solution)/shard_map/bhqk,bqhe->bkhe/dot_general | solution.py:126
  163.2 2.3 %collective-permute-start.13 = (f32[1,16,128,1]{2,1,3,0:T(8,128)S(1)}, f32[1,16,128,1]{2,1,3,0:T(8,128)S(1)}, u32[]{:S(2)}, u32[]{:S(2)}) collective-permute-start(f32[1,16,128,1]{2,1,3,0:T(8,128)S(1)} %bitcast.226), channel_id=1, source_target_pairs={{2,0},{4,2},{6,4},{8,6},{10,8},{12,10},{14,12},{3,1},{5,3},{7,5},{... | collective-permute-start | bytes 24584 | tf_op jit(solution)/shard_map/ppermute | solution.py:16
  165.6 4.3 %collective-permute-start.7 = (f32[1,16,128,1]{2,1,3,0:T(8,128)S(1)}, f32[1,16,128,1]{2,1,3,0:T(8,128)S(1)}, u32[]{:S(2)}, u32[]{:S(2)}) collective-permute-start(f32[1,16,128,1]{2,1,3,0:T(8,128)S(1)} %bitcast.217), channel_id=1, source_target_pairs={{4,0},{6,2},{8,4},{10,6},{12,8},{14,10},{5,1},{7,3},{9,5},{11,7},{... | collective-permute-start | bytes 24584 | tf_op jit(solution)/shard_map/ppermute | solution.py:16
  169.9 2.9 %fusion.14 = f32[16,128,128]{2,1,0:T(8,128)} fusion(bf16[128,16,128]{0,2,1:T(8,128)(2,1)S(1)} %bitcast.199, f32[16,128]{1,0:T(8,128)S(1)} %select_bitcast_fusion.1, f32[16,128]{1,0:T(8,128)S(1)} %bitcast.228, bf16[128,16,128]{2,1,0:T(8,128)(2,1)} %bitcast.206), kind=kOutput, calls=%fused_computation.22 | convolution fusion | flops 67895296 | bytes 2113536 | tf_op jit(solution)/shard_map/bqhe,bkhe->bhqk/dot_general | solution.py:110
  172.7 5.5 %collective-permute-start.6 = (f32[1,16,128,1]{2,1,3,0:T(8,128)S(1)}, f32[1,16,128,1]{2,1,3,0:T(8,128)S(1)}, u32[]{:S(2)}, u32[]{:S(2)}) collective-permute-start(f32[1,16,128,1]{2,1,3,0:T(8,128)S(1)} %bitcast.213), channel_id=1, source_target_pairs={{4,0},{6,2},{8,4},{10,6},{12,8},{14,10},{5,1},{7,3},{9,5},{11,7},{... | collective-permute-start | bytes 24584 | tf_op jit(solution)/shard_map/ppermute | solution.py:16
  178.2 3.0 %fusion.35 = f32[16,128,128]{2,1,0:T(8,128)} fusion(bf16[128,16,128]{0,2,1:T(8,128)(2,1)S(1)} %bitcast.200, bf16[128,16,128]{0,2,1:T(8,128)(2,1)S(1)} %bitcast.185, bf16[128,16,128]{0,2,1:T(8,128)(2,1)S(1)} %bitcast.168, f32[16,128,128]{2,1,0:T(8,128)} %fusion.14, f32[16,128]{1,0:T(8,128)S(1)} %bitcast.218, pred[]{:T(512)} %bitcast.55), kind=kOutput, calls=%fused_computation.60 | convolution fusion | flops 136052736 | bytes 3678209 | tf_op jit(solution)/shard_map/bhqk,bqhe->bkhe/dot_general | solution.py:120
  181.1 2.5 %fusion.46 = f32[16,128,128]{2,1,0:T(8,128)} fusion(bf16[128,16,128]{0,2,1:T(8,128)(2,1)S(1)} %bitcast.186, f32[16,128,128]{2,1,0:T(8,128)} %fusion.14, pred[]{:T(512)} %bitcast.55), kind=kOutput, calls=%fused_computation.71 | convolution fusion | flops 67895296 | bytes 2621441 | tf_op jit(solution)/shard_map/bhqk,bqhe->bkhe/dot_general | solution.py:126
  183.6 1.9 collective-permute-start.8
  185.6 2.1 %fusion.19 = f32[16,128,128]{2,1,0:T(8,128)S(1)} fusion(bf16[128,16,128]{0,2,1:T(8,128)(2,1)} %bitcast.197, f32[16,128]{1,0:T(8,128)S(1)} %select_bitcast_fusion.2, f32[16,128]{1,0:T(8,128)S(1)} %bitcast.230, bf16[128,16,128]{2,1,0:T(8,128)(2,1)} %bitcast.207), kind=kOutput, calls=%fused_computation.29 | convolution fusion | flops 67895296 | bytes 2113536 | tf_op jit(solution)/shard_map/bqhe,bkhe->bhqk/dot_general | solution.py:110
  187.7 2.8 %fusion.34 = f32[16,128,128]{2,1,0:T(8,128)} fusion(bf16[128,16,128]{0,2,1:T(8,128)(2,1)} %bitcast.198, bf16[128,16,128]{0,2,1:T(8,128)(2,1)S(1)} %bitcast.183, bf16[128,16,128]{0,2,1:T(8,128)(2,1)S(1)} %bitcast.169, f32[16,128,128]{2,1,0:T(8,128)S(1)} %fusion.19, f32[16,128]{1,0:T(8,128)S(1)} %bitcast.219, pred[]{:T(512)} %bitcast.47), kind=kOutput, calls=%fused_computation.59 | convolution fusion | flops 136052736 | bytes 3678209 | tf_op jit(solution)/shard_map/bhqk,bqhe->bkhe/dot_general | solution.py:120
  190.5 1.3 fusion.45
  191.8 2.9 %fusion.24 = f32[16,128,128]{2,1,0:T(8,128)} fusion(bf16[128,16,128]{0,2,1:T(8,128)(2,1)S(1)} %bitcast.196, f32[16,128]{1,0:T(8,128)S(1)} %select_bitcast_fusion.3, f32[16,128]{1,0:T(8,128)S(1)} %bitcast.231, bf16[128,16,128]{2,1,0:T(8,128)(2,1)} %bitcast.208), kind=kOutput, calls=%fused_computation.36 | convolution fusion | flops 67895296 | bytes 2113536 | tf_op jit(solution)/shard_map/bqhe,bkhe->bhqk/dot_general | solution.py:110
  194.8 4.0 %fusion.33 = bf16[16,128,128]{2,1,0:T(8,128)(2,1)} fusion(f32[16,128,128]{2,1,0:T(8,128)} %fusion.36, f32[16,128,128]{2,1,0:T(8,128)} %fusion.35, f32[16,128,128]{2,1,0:T(8,128)} %fusion.34, f32[16,128,128]{2,1,0:T(8,128)} %fusion.27, bf16[128,16,128]{0,2,1:T(8,128)(2,1)} %bitcast.195, bf16[128,16,128]{0,2,1:T(8,128)(2,1)S(1)} %bitcast.176, ...), kind=kOutput, calls=%fused_computation.58 | convolution fusion | flops 137363456 | bytes 7348225 | tf_op jit(solution)/shard_map/bhqk,bqhe->bkhe/dot_general | solution.py:120
  198.8 2.0 %copy.63 = bf16[1,128,2048]{2,1,0:T(8,128)(2,1)} copy(bf16[1,128,2048]{1,2,0:T(8,128)(2,1)} %bitcast.192) | data formatting | bytes 1048576
  200.8 1.9 fusion.44
  202.7 1.0 copy.64
  (49 shorter events, 4.7 us)
Async XLA Ops:
  0.6 29.0 %copy-start.3 = (bf16[1,128,2048]{2,1,0:T(8,128)(2,1)S(1)}, bf16[1,128,2048]{2,1,0:T(8,128)(2,1)}, u32[]{:S(2)}) copy-start(bf16[1,128,2048]{2,1,0:T(8,128)(2,1)} %param.7) | copy-start | bytes 1572868
  0.6 21.8 %copy-start.2 = (bf16[1,128,2048]{2,1,0:T(8,128)(2,1)S(1)}, bf16[1,128,2048]{2,1,0:T(8,128)(2,1)}, u32[]{:S(2)}) copy-start(bf16[1,128,2048]{2,1,0:T(8,128)(2,1)} %param.9) | copy-start | bytes 1572868
  4.5 76.2 %collective-permute-start = (bf16[2,1,128,2048]{2,3,1,0:T(8,128)(2,1)}, bf16[2,1,128,2048]{2,3,1,0:T(8,128)(2,1)}, u32[]{:S(2)}, u32[]{:S(2)}) collective-permute-start(bf16[2,1,128,2048]{2,3,1,0:T(8,128)(2,1)} %pad_maximum_fusion), channel_id=1, source_target_pairs={{0,4},{2,6},{4,8},{6,10},{8,12},{10,14},{1,5},{3,7},{5,9},{7,11},{... | collective-permute-start | bytes 3145736 | tf_op jit(solution)/shard_map/ppermute | solution.py:16
  5.7 77.6 %collective-permute-start.1 = (bf16[2,1,128,2048]{2,3,1,0:T(8,128)(2,1)}, bf16[2,1,128,2048]{2,3,1,0:T(8,128)(2,1)}, u32[]{:S(2)}, u32[]{:S(2)}) collective-permute-start(bf16[2,1,128,2048]{2,3,1,0:T(8,128)(2,1)} %pad_maximum_fusion), channel_id=1, source_target_pairs={{0,2},{2,4},{4,6},{6,8},{8,10},{10,12},{12,14},{1,3},{3,5},{5,7},{... | collective-permute-start | bytes 3145736 | tf_op jit(solution)/shard_map/ppermute | solution.py:16
  7.0 82.7 %collective-permute-start.2 = (bf16[2,1,128,2048]{2,3,1,0:T(8,128)(2,1)}, bf16[2,1,128,2048]{2,3,1,0:T(8,128)(2,1)}, u32[]{:S(2)}, u32[]{:S(2)}) collective-permute-start(bf16[2,1,128,2048]{2,3,1,0:T(8,128)(2,1)} %pad_maximum_fusion), channel_id=1, source_target_pairs={{2,0},{4,2},{6,4},{8,6},{10,8},{12,10},{14,12},{3,1},{5,3},{7,5},{... | collective-permute-start | bytes 3145736 | tf_op jit(solution)/shard_map/ppermute | solution.py:16
  12.6 83.1 %collective-permute-start.3 = (bf16[2,1,128,2048]{2,3,1,0:T(8,128)(2,1)}, bf16[2,1,128,2048]{2,3,1,0:T(8,128)(2,1)}, u32[]{:S(2)}, u32[]{:S(2)}) collective-permute-start(bf16[2,1,128,2048]{2,3,1,0:T(8,128)(2,1)} %pad_maximum_fusion), channel_id=1, source_target_pairs={{4,0},{6,2},{8,4},{10,6},{12,8},{14,10},{5,1},{7,3},{9,5},{11,7},{... | collective-permute-start | bytes 3145736 | tf_op jit(solution)/shard_map/ppermute | solution.py:16
  19.8 34.1 %collective-permute-start.20 = (s32[1]{0:T(128)}, s32[1]{0:T(128)}, u32[]{:S(2)}, u32[]{:S(2)}) collective-permute-start(s32[1]{0:T(128)} %bitcast.61), channel_id=1, source_target_pairs={{0,4},{2,6},{4,8},{6,10},{8,12},{10,14},{1,5},{3,7},{5,9},{7,11},{... | collective-permute-start | bytes 20 | tf_op jit(solution)/shard_map/ppermute | solution.py:16
  29.7 60.1 %copy-start.7 = (bf16[2,1,128,2048]{2,3,1,0:T(8,128)(2,1)S(1)}, bf16[2,1,128,2048]{2,3,1,0:T(8,128)(2,1)}, u32[]{:S(2)}) copy-start(bf16[2,1,128,2048]{2,3,1,0:T(8,128)(2,1)} %pad_maximum_fusion.1) | copy-start | bytes 3145732
  53.9 5.5 %collective-permute-start.15 = (s32[1]{0:T(128)}, s32[1]{0:T(128)}, u32[]{:S(2)}, u32[]{:S(2)}) collective-permute-start(s32[1]{0:T(128)} %bitcast.54), channel_id=1, source_target_pairs={{0,2},{2,4},{4,6},{6,8},{8,10},{10,12},{12,14},{1,3},{3,5},{5,7},{... | collective-permute-start | bytes 20 | tf_op jit(solution)/shard_map/ppermute | solution.py:16
  59.4 12.4 %collective-permute-start.10 = (s32[1]{0:T(128)}, s32[1]{0:T(128)}, u32[]{:S(2)}, u32[]{:S(2)}) collective-permute-start(s32[1]{0:T(128)} %bitcast.46), channel_id=1, source_target_pairs={{2,0},{4,2},{6,4},{8,6},{10,8},{12,10},{14,12},{3,1},{5,3},{7,5},{... | collective-permute-start | bytes 20 | tf_op jit(solution)/shard_map/ppermute | solution.py:16
  71.9 6.9 %collective-permute-start.5 = (s32[1]{0:T(128)}, s32[1]{0:T(128)}, u32[]{:S(2)}, u32[]{:S(2)}) collective-permute-start(s32[1]{0:T(128)} %bitcast.34), channel_id=1, source_target_pairs={{4,0},{6,2},{8,4},{10,6},{12,8},{14,10},{5,1},{7,3},{9,5},{11,7},{... | collective-permute-start | bytes 20 | tf_op jit(solution)/shard_map/ppermute | solution.py:16
  78.8 29.9 %collective-permute-start.19 = (bf16[2,1,128,2048]{2,3,1,0:T(8,128)(2,1)}, bf16[2,1,128,2048]{2,3,1,0:T(8,128)(2,1)S(1)}, u32[]{:S(2)}, u32[]{:S(2)}) collective-permute-start(bf16[2,1,128,2048]{2,3,1,0:T(8,128)(2,1)} %pad_maximum_fusion.1), channel_id=1, source_target_pairs={{0,4},{2,6},{4,8},{6,10},{8,12},{10,14},{1,5},{3,7},{5,9},{7,11},{... | collective-permute-start | bytes 3145736 | tf_op jit(solution)/shard_map/ppermute | solution.py:16
  80.6 30.2 %collective-permute-start.14 = (bf16[2,1,128,2048]{2,3,1,0:T(8,128)(2,1)}, bf16[2,1,128,2048]{2,3,1,0:T(8,128)(2,1)S(1)}, u32[]{:S(2)}, u32[]{:S(2)}) collective-permute-start(bf16[2,1,128,2048]{2,3,1,0:T(8,128)(2,1)} %pad_maximum_fusion.1), channel_id=1, source_target_pairs={{0,2},{2,4},{4,6},{6,8},{8,10},{10,12},{12,14},{1,3},{3,5},{5,7},{... | collective-permute-start | bytes 3145736 | tf_op jit(solution)/shard_map/ppermute | solution.py:16
  83.3 45.7 %collective-permute-start.9 = (bf16[2,1,128,2048]{2,3,1,0:T(8,128)(2,1)}, bf16[2,1,128,2048]{2,3,1,0:T(8,128)(2,1)S(1)}, u32[]{:S(2)}, u32[]{:S(2)}) collective-permute-start(bf16[2,1,128,2048]{2,3,1,0:T(8,128)(2,1)} %pad_maximum_fusion.1), channel_id=1, source_target_pairs={{2,0},{4,2},{6,4},{8,6},{10,8},{12,10},{14,12},{3,1},{5,3},{7,5},{... | collective-permute-start | bytes 3145736 | tf_op jit(solution)/shard_map/ppermute | solution.py:16
  89.7 44.7 %collective-permute-start.4 = (bf16[2,1,128,2048]{2,3,1,0:T(8,128)(2,1)S(1)}, bf16[2,1,128,2048]{2,3,1,0:T(8,128)(2,1)S(1)}, u32[]{:S(2)}, u32[]{:S(2)}) collective-permute-start(bf16[2,1,128,2048]{2,3,1,0:T(8,128)(2,1)S(1)} %copy-done.7), channel_id=1, source_target_pairs={{4,0},{6,2},{8,4},{10,6},{12,8},{14,10},{5,1},{7,3},{9,5},{11,7},{... | collective-permute-start | bytes 3145736 | tf_op jit(solution)/shard_map/ppermute | solution.py:16
  97.7 2.6 %copy-start.6 = (f32[1,128,2048]{1,2,0:T(8,128)S(1)}, f32[1,128,2048]{1,2,0:T(8,128)}, u32[]{:S(2)}) copy-start(f32[1,128,2048]{1,2,0:T(8,128)} %copy.45) | copy-start | bytes 3145732
  107.4 34.8 %collective-permute-start.22 = (f32[1,16,128,1]{2,1,3,0:T(8,128)S(1)}, f32[1,16,128,1]{2,1,3,0:T(8,128)S(1)}, u32[]{:S(2)}, u32[]{:S(2)}) collective-permute-start(f32[1,16,128,1]{2,1,3,0:T(8,128)S(1)} %bitcast.214), channel_id=1, source_target_pairs={{0,4},{2,6},{4,8},{6,10},{8,12},{10,14},{1,5},{3,7},{5,9},{7,11},{... | collective-permute-start | bytes 24584 | tf_op jit(solution)/shard_map/ppermute | solution.py:16
  108.7 54.5 %collective-permute-start.17 = (f32[1,16,128,1]{2,1,3,0:T(8,128)S(1)}, f32[1,16,128,1]{2,1,3,0:T(8,128)S(1)}, u32[]{:S(2)}, u32[]{:S(2)}) collective-permute-start(f32[1,16,128,1]{2,1,3,0:T(8,128)S(1)} %bitcast.215), channel_id=1, source_target_pairs={{0,2},{2,4},{4,6},{6,8},{8,10},{10,12},{12,14},{1,3},{3,5},{5,7},{... | collective-permute-start | bytes 24584 | tf_op jit(solution)/shard_map/ppermute | solution.py:16
  110.9 32.6 %collective-permute-start.21 = (f32[1,16,128,1]{2,1,3,0:T(8,128)S(1)}, f32[1,16,128,1]{2,1,3,0:T(8,128)S(1)}, u32[]{:S(2)}, u32[]{:S(2)}) collective-permute-start(f32[1,16,128,1]{2,1,3,0:T(8,128)S(1)} %bitcast.210), channel_id=1, source_target_pairs={{0,4},{2,6},{4,8},{6,10},{8,12},{10,14},{1,5},{3,7},{5,9},{7,11},{... | collective-permute-start | bytes 24584 | tf_op jit(solution)/shard_map/ppermute | solution.py:16
  129.0 36.6 %collective-permute-start.16 = (f32[1,16,128,1]{2,1,3,0:T(8,128)S(1)}, f32[1,16,128,1]{2,1,3,0:T(8,128)S(1)}, u32[]{:S(2)}, u32[]{:S(2)}) collective-permute-start(f32[1,16,128,1]{2,1,3,0:T(8,128)S(1)} %bitcast.211), channel_id=1, source_target_pairs={{0,2},{2,4},{4,6},{6,8},{8,10},{10,12},{12,14},{1,3},{3,5},{5,7},{... | collective-permute-start | bytes 24584 | tf_op jit(solution)/shard_map/ppermute | solution.py:16
  140.9 11.3 %collective-permute-start.23 = (f32[1,16,128,1]{2,1,3,0:T(8,128)S(1)}, f32[1,16,128,1]{2,1,3,0:T(8,128)S(1)}, u32[]{:S(2)}, u32[]{:S(2)}) collective-permute-start(f32[1,16,128,1]{2,1,3,0:T(8,128)S(1)} %bitcast.224), channel_id=1, source_target_pairs={{0,4},{2,6},{4,8},{6,10},{8,12},{10,14},{1,5},{3,7},{5,9},{7,11},{... | collective-permute-start | bytes 24584 | tf_op jit(solution)/shard_map/ppermute | solution.py:16
  142.2 30.6 %collective-permute-start.18 = (f32[1,16,128,1]{2,1,3,0:T(8,128)S(1)}, f32[1,16,128,1]{2,1,3,0:T(8,128)S(1)}, u32[]{:S(2)}, u32[]{:S(2)}) collective-permute-start(f32[1,16,128,1]{2,1,3,0:T(8,128)S(1)} %bitcast.225), channel_id=1, source_target_pairs={{0,2},{2,4},{4,6},{6,8},{8,10},{10,12},{12,14},{1,3},{3,5},{5,7},{... | collective-permute-start | bytes 24584 | tf_op jit(solution)/shard_map/ppermute | solution.py:16
  143.5 40.2 %collective-permute-start.12 = (f32[1,16,128,1]{2,1,3,0:T(8,128)S(1)}, f32[1,16,128,1]{2,1,3,0:T(8,128)S(1)}, u32[]{:S(2)}, u32[]{:S(2)}) collective-permute-start(f32[1,16,128,1]{2,1,3,0:T(8,128)S(1)} %bitcast.216), channel_id=1, source_target_pairs={{2,0},{4,2},{6,4},{8,6},{10,8},{12,10},{14,12},{3,1},{5,3},{7,5},{... | collective-permute-start | bytes 24584 | tf_op jit(solution)/shard_map/ppermute | solution.py:16
  149.1 20.8 %copy-start.5 = (bf16[1,1,128,2048]{2,3,1,0:T(8,128)(2,1)S(1)}, bf16[1,1,128,2048]{2,3,1,0:T(8,128)(2,1)}, u32[]{:S(2)}) copy-start(bf16[1,1,128,2048]{2,3,1,0:T(8,128)(2,1)} %get-tuple-element.23) | copy-start | bytes 1572868
  152.2 33.4 %collective-permute-start.11 = (f32[1,16,128,1]{2,1,3,0:T(8,128)S(1)}, f32[1,16,128,1]{2,1,3,0:T(8,128)S(1)}, u32[]{:S(2)}, u32[]{:S(2)}) collective-permute-start(f32[1,16,128,1]{2,1,3,0:T(8,128)S(1)} %bitcast.212), channel_id=1, source_target_pairs={{2,0},{4,2},{6,4},{8,6},{10,8},{12,10},{14,12},{3,1},{5,3},{7,5},{... | collective-permute-start | bytes 24584 | tf_op jit(solution)/shard_map/ppermute | solution.py:16
  163.2 24.5 %collective-permute-start.13 = (f32[1,16,128,1]{2,1,3,0:T(8,128)S(1)}, f32[1,16,128,1]{2,1,3,0:T(8,128)S(1)}, u32[]{:S(2)}, u32[]{:S(2)}) collective-permute-start(f32[1,16,128,1]{2,1,3,0:T(8,128)S(1)} %bitcast.226), channel_id=1, source_target_pairs={{2,0},{4,2},{6,4},{8,6},{10,8},{12,10},{14,12},{3,1},{5,3},{7,5},{... | collective-permute-start | bytes 24584 | tf_op jit(solution)/shard_map/ppermute | solution.py:16
  165.6 26.2 %collective-permute-start.7 = (f32[1,16,128,1]{2,1,3,0:T(8,128)S(1)}, f32[1,16,128,1]{2,1,3,0:T(8,128)S(1)}, u32[]{:S(2)}, u32[]{:S(2)}) collective-permute-start(f32[1,16,128,1]{2,1,3,0:T(8,128)S(1)} %bitcast.217), channel_id=1, source_target_pairs={{4,0},{6,2},{8,4},{10,6},{12,8},{14,10},{5,1},{7,3},{9,5},{11,7},{... | collective-permute-start | bytes 24584 | tf_op jit(solution)/shard_map/ppermute | solution.py:16
  172.7 19.1 %collective-permute-start.6 = (f32[1,16,128,1]{2,1,3,0:T(8,128)S(1)}, f32[1,16,128,1]{2,1,3,0:T(8,128)S(1)}, u32[]{:S(2)}, u32[]{:S(2)}) collective-permute-start(f32[1,16,128,1]{2,1,3,0:T(8,128)S(1)} %bitcast.213), channel_id=1, source_target_pairs={{4,0},{6,2},{8,4},{10,6},{12,8},{14,10},{5,1},{7,3},{9,5},{11,7},{... | collective-permute-start | bytes 24584 | tf_op jit(solution)/shard_map/ppermute | solution.py:16
  183.6 11.1 %collective-permute-start.8 = (f32[1,16,128,1]{2,1,3,0:T(8,128)S(1)}, f32[1,16,128,1]{2,1,3,0:T(8,128)S(1)}, u32[]{:S(2)}, u32[]{:S(2)}) collective-permute-start(f32[1,16,128,1]{2,1,3,0:T(8,128)S(1)} %bitcast.227), channel_id=1, source_target_pairs={{4,0},{6,2},{8,4},{10,6},{12,8},{14,10},{5,1},{7,3},{9,5},{11,7},{... | collective-permute-start | bytes 24584 | tf_op jit(solution)/shard_map/ppermute | solution.py:16
  185.6 6.2 %copy-start.4 = (bf16[1,1,128,2048]{2,3,1,0:T(8,128)(2,1)S(1)}, bf16[1,1,128,2048]{2,3,1,0:T(8,128)(2,1)}, u32[]{:S(2)}) copy-start(bf16[1,1,128,2048]{2,3,1,0:T(8,128)(2,1)} %get-tuple-element.19) | copy-start | bytes 1572868
  194.8 6.1 %copy-start = (f32[16,128,128]{2,1,0:T(8,128)S(1)}, f32[16,128,128]{2,1,0:T(8,128)}, u32[]{:S(2)}) copy-start(f32[16,128,128]{2,1,0:T(8,128)} %fusion.38) | copy-start | bytes 3145732
  194.8 6.1 %copy-start.1 = (f32[16,128,128]{2,1,0:T(8,128)S(1)}, f32[16,128,128]{2,1,0:T(8,128)}, u32[]{:S(2)}) copy-start(f32[16,128,128]{2,1,0:T(8,128)} %fusion.47) | copy-start | bytes 3145732
where the time goes:
time: 205 us; the launch traced here: 204 us
  starting transfers between devices  77.9 us (38%)
  matrix products  43.5 us (21%)
  waiting for transfers between devices  42.9 us (21%)
  local copies, waits for them, and re-layouts  26.1 us (13%)
  between operations  6.92 us (3%)
  other arithmetic  6.56 us (3%)
    ppermute x24, starting transfers between devices, passed_along(): return lax.ppermute(array, axis, pairs)  77.9 us
    ppermute x24, waiting for transfers between devices, passed_along(): return lax.ppermute(array, axis, pairs)  42.9 us
    unnamed x26, local copies, waits for them, and re-layouts  15.1 us
    dot_general x4, matrix products, local(): jnp.einsum('bhqk,bqhe->bkhe', far_dscore, far_query, preferred_element_ty...  12.9 us
    dot_general x4, matrix products, local(): jnp.einsum('bqhe,bkhe->bhqk', far_query, own_keys, preferred_element_type...  11 us
    dot_general x4, matrix products, local(): jnp.einsum('bhqk,bqhe->bkhe', far_low, far_grad, preferred_element_type=j...  8.14 us
  transfers between devices with their start and end apart: 24, of which 3 were waited for; matrix products, arithmetic and copies ran while one was open for 31% of the time, Pallas kernels for 0%

commit v1 on v0

v1 whole, which is shorter than its diff:
```python
import functools

import jax
import jax.numpy as jnp
from jax import lax
from jax.experimental import pallas as pl
from jax.experimental.pallas import tpu as pltpu
from jax.sharding import PartitionSpec as P

HEADS = 16
HEAD_DIM = 128
TILE = 128
REACH = 2
MAXN = 4
HALF = HEADS // 2
SLOTS = 6
AHEAD = 2
BEHIND = 1
INV_ROOT = HEAD_DIM ** (-0.5)
MESH = pl.DeviceIdType.MESH


def nt(a, b):
    return lax.dot_general(a, b, (((1,), (1,)), ((), ())), preferred_element_type=jnp.float32)


def nn(a, b):
    return jnp.dot(a, b, preferred_element_type=jnp.float32)


def kernel(
    peers,
    neighbours_ref, counts_ref, q_ref, k_ref, v_ref, g_ref,
    att_ref, gq_ref, gk_ref, gv_ref,
    kv, qg, share_out, share_in, result, own, bias,
    send_sem, recv_sem, local_sem, bias_sem,
):
    me = lax.axis_index("mp")
    side = lax.rem(me, 2)
    other = 1 - side
    partner = me + 1 - 2 * side
    pair = lax.div(me, 2)
    has_up = me + 2 < peers
    has_down = me >= 2
    up = me + 2
    down = me - 2
    width = HALF * HEAD_DIM

    def columns(half, h):
        return pl.ds(pl.multiple_of(half * width + h * HEAD_DIM, HEAD_DIM), HEAD_DIM)

    def remote(src, dst, stream, h, target):
        return pltpu.make_async_remote_copy(
            src_ref=src,
            dst_ref=dst,
            send_sem=send_sem.at[h, stream],
            recv_sem=recv_sem.at[h, stream],
            device_id={"mp": target},
            device_id_type=MESH,
        )

    inputs = (k_ref, v_ref, q_ref, g_ref)
    outputs = (att_ref, gq_ref, gk_ref, gv_ref)

    def place(i, h, which):
        return kv.at[h, 1, which, i] if i < 2 else qg.at[h, which, i - 2]

    def give(i, h):
        return remote(
            inputs[i].at[0, :, columns(other, h)], place(i, h, side), i, h, partner
        )

    def take(i, h):
        return remote(
            inputs[i].at[0, :, columns(other, h)], place(i, h, other), i, h, partner
        )

    def keep(i, h):
        return pltpu.make_async_copy(
            inputs[i].at[0, :, columns(side, h)], place(i, h, side), local_sem.at[h, i]
        )

    def own_up(i, h):
        return remote(inputs[i].at[0, :, columns(side, h)], kv.at[h, 0, side, i], 4 + i, h, up)

    def own_down(i, h):
        return remote(inputs[i].at[0, :, columns(side, h)], kv.at[h, 2, side, i], 6 + i, h, down)

    def pass_up(h):
        return remote(kv.at[h, 1, other], kv.at[h, 0, other], 8, h, up)

    def pass_down(h):
        return remote(kv.at[h, 1, other], kv.at[h, 2, other], 9, h, down)

    def share_up(h):
        return remote(share_out.at[h, 1], share_in.at[h, 0], 10, h, up)

    def share_down(h):
        return remote(share_out.at[h, 0], share_in.at[h, 1], 11, h, down)

    def hand_back(i, h):
        return remote(
            result.at[h, other, i], outputs[i].at[0, :, columns(side, h)], 12 + i, h, partner
        )

    def take_back(i, h):
        return remote(
            result.at[h, other, i], outputs[i].at[0, :, columns(other, h)], 12 + i, h, partner
        )

    def write(i, h):
        return pltpu.make_async_copy(
            result.at[h, side, i], outputs[i].at[0, :, columns(side, h)], local_sem.at[h, 4 + i]
        )

    def bias_copy(which):
        return pltpu.make_async_remote_copy(
            src_ref=bias.at[side],
            dst_ref=bias.at[which],
            send_sem=bias_sem.at[0],
            recv_sem=bias_sem.at[1],
            device_id={"mp": partner},
            device_id_type=MESH,
        )

    barrier = pltpu.get_barrier_semaphore()
    pl.semaphore_signal(barrier, inc=1, device_id={"mp": partner}, device_id_type=MESH)

    @pl.when(has_up)
    def _():
        pl.semaphore_signal(barrier, inc=1, device_id={"mp": up}, device_id_type=MESH)

    @pl.when(has_down)
    def _():
        pl.semaphore_signal(barrier, inc=1, device_id={"mp": down}, device_id_type=MESH)

    @pl.loop(0, HALF)
    def _(h):
        for i in range(4):
            keep(i, h).start()

    tile = 2 * pair - 2 + lax.broadcasted_iota(jnp.int32, (8, TILE), 0)
    present = tile == me
    listed_count = counts_ref[0, 0]
    near = (tile >= me - REACH) & (tile <= me + REACH)
    for place_at in range(MAXN):
        wanted = neighbours_ref[0, 0, place_at]
        wanted = jnp.where(place_at < listed_count, wanted, -1000)
        present = present | (near & (tile == wanted))
    bias[side] = jnp.where(present, 0.0, -jnp.inf).astype(jnp.float32)

    pl.semaphore_wait(barrier, 1 + has_up.astype(jnp.int32) + has_down.astype(jnp.int32))

    bias_copy(side).start()

    @pl.loop(0, HALF)
    def _(h):
        give(0, h).start()
        give(1, h).start()

        @pl.when(has_up)
        def _():
            own_up(0, h).start()
            own_up(1, h).start()

        @pl.when(has_down)
        def _():
            own_down(0, h).start()
            own_down(1, h).start()

        give(2, h).start()
        give(3, h).start()


    def clear(ref, slot):
        @pl.loop(0, HALF)
        def _(h):
            ref[h, slot] = jnp.zeros((2, 2, TILE, HEAD_DIM), jnp.bfloat16)

    @pl.when(jnp.logical_not(has_down))
    def _():
        clear(kv, 0)
        clear(share_in, 0)

    @pl.when(jnp.logical_not(has_up))
    def _():
        clear(kv, 2)
        clear(share_in, 1)

    def forward(h):
        take(0, h).wait_recv()
        take(1, h).wait_recv()

        @pl.when(has_up)
        def _():
            pass_up(h).start()

        @pl.when(has_down)
        def _():
            pass_down(h).start()

    def gather(h):
        for i in range(4):
            keep(i, h).wait()
        take(2, h).wait_recv()
        take(3, h).wait_recv()

        @pl.when(has_down)
        def _():
            own_up(0, h).wait_recv()
            own_up(1, h).wait_recv()
            pass_up(h).wait_recv()

        @pl.when(has_up)
        def _():
            own_down(0, h).wait_recv()
            own_down(1, h).wait_recv()
            pass_down(h).wait_recv()

    def attend(h):
        query = qg[h, :, 0].reshape(2 * TILE, HEAD_DIM)
        grad = qg[h, :, 1].reshape(2 * TILE, HEAD_DIM)
        keys = [kv[h, s // 2, s % 2, 0] for s in range(SLOTS)]
        values = [kv[h, s // 2, s % 2, 1] for s in range(SLOTS)]
        scores = []
        for s in range(SLOTS):
            row = jnp.concatenate([bias[0, s : s + 1, :], bias[1, s : s + 1, :]], axis=1)
            scores.append(nt(keys[s], query) * INV_ROOT + row)
        top = scores[0]
        for s in range(1, SLOTS):
            top = jnp.maximum(top, scores[s])
        top = jnp.max(top, axis=0, keepdims=True)
        powers = [jnp.exp(score - top) for score in scores]
        total = powers[0]
        for s in range(1, SLOTS):
            total = total + powers[s]
        scale = 1.0 / jnp.sum(total, axis=0, keepdims=True)
        weights = [power * scale for power in powers]
        low = [weight.astype(jnp.bfloat16) for weight in weights]
        prob = [nt(values[s], grad) for s in range(SLOTS)]
        delta = low[0].astype(jnp.float32) * prob[0]
        for s in range(1, SLOTS):
            delta = delta + low[s].astype(jnp.float32) * prob[s]
        delta = jnp.sum(delta, axis=0, keepdims=True)
        dscore = [
            (weights[s] * (prob[s] - delta) * INV_ROOT).astype(jnp.bfloat16) for s in range(SLOTS)
        ]
        mixture = jnp.zeros((HEAD_DIM, 2 * TILE), jnp.float32)
        grad_query = jnp.zeros((HEAD_DIM, 2 * TILE), jnp.float32)
        for s in range(SLOTS):
            key_share = nn(dscore[s], query)
            value_share = nn(low[s], grad)
            if s // 2 == 1:
                own[h, s % 2, 0] = key_share
                own[h, s % 2, 1] = value_share
            else:
                share_out[h, s // 4, s % 2, 0] = key_share.astype(jnp.bfloat16)
                share_out[h, s // 4, s % 2, 1] = value_share.astype(jnp.bfloat16)
            mixture = mixture + nn(values[s].T, low[s])
            grad_query = grad_query + nn(keys[s].T, dscore[s])
        mixture = mixture.T.astype(jnp.bfloat16)
        grad_query = grad_query.T.astype(jnp.bfloat16)
        for which in range(2):
            rows = slice(which * TILE, (which + 1) * TILE)
            result[h, which, 0] = mixture[rows]
            result[h, which, 1] = grad_query[rows]

    def finish(h):
        @pl.when(has_down)
        def _():
            share_up(h).wait_recv()

        @pl.when(has_up)
        def _():
            share_down(h).wait_recv()

        total = (
            own[h]
            + share_in[h, 0].astype(jnp.float32)
            + share_in[h, 1].astype(jnp.float32)
        ).astype(jnp.bfloat16)
        for which in range(2):
            result[h, which, 2] = total[which, 0]
            result[h, which, 3] = total[which, 1]
        for i in range(2, 4):
            hand_back(i, h).start()
            write(i, h).start()

    for h in range(AHEAD):
        forward(h)
    bias_copy(other).wait_recv()

    @pl.loop(0, HALF)
    def _(h):
        @pl.when(h + AHEAD < HALF)
        def _():
            forward(h + AHEAD)

        gather(h)
        attend(h)

        @pl.when(has_up)
        def _():
            share_up(h).start()

        @pl.when(has_down)
        def _():
            share_down(h).start()

        for i in range(2):
            hand_back(i, h).start()
            write(i, h).start()

        @pl.when(h >= BEHIND)
        def _():
            finish(h - BEHIND)

    for h in range(HALF - BEHIND, HALF):
        finish(h)

    bias_copy(side).wait_send()

    @pl.loop(0, HALF)
    def _(h):
        for i in range(4):
            give(i, h).wait_send()
            write(i, h).wait()
            take_back(i, h).wait_recv()
            hand_back(i, h).wait_send()

        @pl.when(has_up)
        def _():
            own_up(0, h).wait_send()
            own_up(1, h).wait_send()
            pass_up(h).wait_send()
            share_up(h).wait_send()

        @pl.when(has_down)
        def _():
            own_down(0, h).wait_send()
            own_down(1, h).wait_send()
            pass_down(h).wait_send()
            share_down(h).wait_send()


def local(peers, queries, keys, values, grad_out, neighbours, counts):
    rows, tokens, features = queries.shape
    anywhere = pl.BlockSpec(memory_space=pl.ANY)
    scalars = pl.BlockSpec(memory_space=pltpu.SMEM)
    out = jax.ShapeDtypeStruct((rows, tokens, features), jnp.bfloat16)
    return tuple(
        pl.pallas_call(
            functools.partial(kernel, peers),
            out_shape=(out, out, out, out),
            in_specs=[scalars, scalars, anywhere, anywhere, anywhere, anywhere],
            out_specs=(anywhere, anywhere, anywhere, anywhere),
            scratch_shapes=[
                pltpu.VMEM((HALF, 3, 2, 2, TILE, HEAD_DIM), jnp.bfloat16),
                pltpu.VMEM((HALF, 2, 2, TILE, HEAD_DIM), jnp.bfloat16),
                pltpu.VMEM((HALF, 2, 2, 2, TILE, HEAD_DIM), jnp.bfloat16),
                pltpu.VMEM((HALF, 2, 2, 2, TILE, HEAD_DIM), jnp.bfloat16),
                pltpu.VMEM((HALF, 2, 4, TILE, HEAD_DIM), jnp.bfloat16),
                pltpu.VMEM((HALF, 2, 2, TILE, HEAD_DIM), jnp.float32),
                pltpu.VMEM((2, 8, TILE), jnp.float32),
                pltpu.SemaphoreType.DMA((HALF, 16)),
                pltpu.SemaphoreType.DMA((HALF, 16)),
                pltpu.SemaphoreType.DMA((HALF, 8)),
                pltpu.SemaphoreType.DMA((2,)),
            ],
            compiler_params=pltpu.CompilerParams(
                collective_id=0, has_side_effects=True, vmem_limit_bytes=40 * 1024 * 1024
            ),
            cost_estimate=pl.CostEstimate(
                flops=2_500_000_000, bytes_accessed=4_194_304, transcendentals=1_600_000
            ),
        )(neighbours, counts, queries, keys, values, grad_out)
    )


def solution(mesh):
    spec = P(("groups", "dp"), "mp", None)
    return jax.shard_map(
        functools.partial(local, mesh.shape["mp"]),
        mesh=mesh,
        in_specs=(spec, spec, spec, spec, spec, P(("groups", "dp"), "mp")),
        out_specs=(spec, spec, spec, spec),
        check_vma=False,
    )
```

time: 205 us -> 68.1 us (0.33)
  the two profiles are of different devices: /device:TPU:30 before, /device:TPU:0 now
where the time goes in v1:
time: 68.1 us; the launch traced here: 67.8 us
  Pallas kernels  59.1 us (87%)
  local copies, waits for them, and re-layouts  7.34 us (11%)
  between operations  1.33 us (2%)
    pallas_call x1, Pallas kernels, local(): pl.pallas_call(functools.partial(kernel, peers), out_shape=(out, out, out...  59.1 us
    unnamed x14, local copies, waits for them, and re-layouts  7.34 us

profile of v1, /device:TPU:0, one launch (start us, length us, event | category | flops | bytes accessed | tf_op | source)
XLA Modules:
  0.0 67.8 jit_solution(18428351002564672296)
XLA Ops:
  0.6 0.0 copy-start.4
  1.3 0.0 copy-done.4
  1.3 0.0 copy-start
  1.3 1.0 %copy-done = bf16[1,128,2048]{2,1,0:T(8,128)(2,1)S(1)} copy-done((bf16[1,128,2048]{2,1,0:T(8,128)(2,1)S(1)}, bf16[1,128,2048]{2,1,0:T(8,128)(2,1)}, u32[]{:S(2)}) %copy-start) | copy-done | bytes 524312
  2.4 0.0 copy-start.1
  2.4 1.0 %copy-done.1 = bf16[1,128,2048]{2,1,0:T(8,128)(2,1)S(1)} copy-done((bf16[1,128,2048]{2,1,0:T(8,128)(2,1)S(1)}, bf16[1,128,2048]{2,1,0:T(8,128)(2,1)}, u32[]{:S(2)}) %copy-start.1) | copy-done | bytes 524312
  3.4 0.0 copy-start.2
  3.4 1.0 %copy-done.2 = bf16[1,128,2048]{2,1,0:T(8,128)(2,1)S(1)} copy-done((bf16[1,128,2048]{2,1,0:T(8,128)(2,1)S(1)}, bf16[1,128,2048]{2,1,0:T(8,128)(2,1)}, u32[]{:S(2)}) %copy-start.2) | copy-done | bytes 524312
  4.4 0.0 copy-start.3
  4.4 1.0 %copy-done.3 = bf16[1,128,2048]{2,1,0:T(8,128)(2,1)S(1)} copy-done((bf16[1,128,2048]{2,1,0:T(8,128)(2,1)S(1)}, bf16[1,128,2048]{2,1,0:T(8,128)(2,1)}, u32[]{:S(2)}) %copy-start.3) | copy-done | bytes 524312
  5.5 59.1 %shard_map.93 = (bf16[1,128,2048]{2,1,0:T(8,128)(2,1)S(1)}, bf16[1,128,2048]{2,1,0:T(8,128)(2,1)S(1)}, bf16[1,128,2048]{2,1,0:T(8,128)(2,1)S(1)}, bf16[1,128,2048]{2,1,0:T(8,128)(2,1)S(1)}) custom-call(s32[1,1,4]{2,1,0:T(1,128)S(1)} %copy-done.4, s32[1,1]{1,0:T(1,128)S(6)} %copy.14.counts_ref, bf16[1,128,2048]{2,1,0:T(8,128)(2,1)S(1)} %copy-done, ...), custom_call_target="tpu_custom_call" | custom-call | flops 2500000000 | bytes 4194304 | tf_op jit(solution)/shard_map/pallas_call | solution.py:352
  64.6 0.8 %copy.15 = bf16[1,128,2048]{2,1,0:T(8,128)(2,1)} copy(bf16[1,128,2048]{2,1,0:T(8,128)(2,1)S(1)} %get-tuple-element.8) | data formatting | bytes 1048576
  65.4 0.8 %copy.16 = bf16[1,128,2048]{2,1,0:T(8,128)(2,1)} copy(bf16[1,128,2048]{2,1,0:T(8,128)(2,1)S(1)} %get-tuple-element.9) | data formatting | bytes 1048576
  66.2 0.8 %copy.17 = bf16[1,128,2048]{2,1,0:T(8,128)(2,1)} copy(bf16[1,128,2048]{2,1,0:T(8,128)(2,1)S(1)} %get-tuple-element.10) | data formatting | bytes 1048576
  67.0 0.8 %copy.18 = bf16[1,128,2048]{2,1,0:T(8,128)(2,1)} copy(bf16[1,128,2048]{2,1,0:T(8,128)(2,1)S(1)} %get-tuple-element.11) | data formatting | bytes 1048576
Async XLA Ops:
  0.6 0.7 copy-start.4
  1.3 1.0 %copy-start = (bf16[1,128,2048]{2,1,0:T(8,128)(2,1)S(1)}, bf16[1,128,2048]{2,1,0:T(8,128)(2,1)}, u32[]{:S(2)}) copy-start(bf16[1,128,2048]{2,1,0:T(8,128)(2,1)} %q_ref.1) | copy-start | bytes 1572868
  2.4 1.0 %copy-start.1 = (bf16[1,128,2048]{2,1,0:T(8,128)(2,1)S(1)}, bf16[1,128,2048]{2,1,0:T(8,128)(2,1)}, u32[]{:S(2)}) copy-start(bf16[1,128,2048]{2,1,0:T(8,128)(2,1)} %k_ref.1) | copy-start | bytes 1572868
  3.4 1.0 %copy-start.2 = (bf16[1,128,2048]{2,1,0:T(8,128)(2,1)S(1)}, bf16[1,128,2048]{2,1,0:T(8,128)(2,1)}, u32[]{:S(2)}) copy-start(bf16[1,128,2048]{2,1,0:T(8,128)(2,1)} %v_ref.1) | copy-start | bytes 1572868
  4.4 1.0 %copy-start.3 = (bf16[1,128,2048]{2,1,0:T(8,128)(2,1)S(1)}, bf16[1,128,2048]{2,1,0:T(8,128)(2,1)}, u32[]{:S(2)}) copy-start(bf16[1,128,2048]{2,1,0:T(8,128)(2,1)} %g_ref.1) | copy-start | bytes 1572868

commit v2 on v1

--- a/solution.py
+++ b/solution.py
@@ -15,7 +15,7 @@
 HALF = HEADS // 2
 SLOTS = 6
 AHEAD = 2
-BEHIND = 1
+BEHIND = 2
 INV_ROOT = HEAD_DIM ** (-0.5)
 MESH = pl.DeviceIdType.MESH
 
@@ -343,13 +343,25 @@
             share_down(h).wait_send()
 
 
+def settle(*refs):
+    sources, targets, staged, sem = refs[:4], refs[4:8], refs[8], refs[9]
+    reads = [pltpu.make_async_copy(sources[i], staged.at[i], sem.at[0, i]) for i in range(4)]
+    writes = [pltpu.make_async_copy(staged.at[i], targets[i], sem.at[1, i]) for i in range(4)]
+    for read in reads:
+        read.start()
+    for read, write in zip(reads, writes):
+        read.wait()
+        write.start()
+    for write in writes:
+        write.wait()
+
+
 def local(peers, queries, keys, values, grad_out, neighbours, counts):
     rows, tokens, features = queries.shape
     anywhere = pl.BlockSpec(memory_space=pl.ANY)
     scalars = pl.BlockSpec(memory_space=pltpu.SMEM)
     out = jax.ShapeDtypeStruct((rows, tokens, features), jnp.bfloat16)
-    return tuple(
-        pl.pallas_call(
+    packed = pl.pallas_call(
             functools.partial(kernel, peers),
             out_shape=(out, out, out, out),
             in_specs=[scalars, scalars, anywhere, anywhere, anywhere, anywhere],
@@ -368,12 +380,23 @@
                 pltpu.SemaphoreType.DMA((2,)),
             ],
             compiler_params=pltpu.CompilerParams(
-                collective_id=0, has_side_effects=True, vmem_limit_bytes=40 * 1024 * 1024
+                collective_id=0, has_side_effects=True, vmem_limit_bytes=60 * 1024 * 1024
             ),
             cost_estimate=pl.CostEstimate(
                 flops=2_500_000_000, bytes_accessed=4_194_304, transcendentals=1_600_000
             ),
         )(neighbours, counts, queries, keys, values, grad_out)
+    return tuple(
+        pl.pallas_call(
+            settle,
+            out_shape=(out, out, out, out),
+            in_specs=[anywhere] * 4,
+            out_specs=(anywhere,) * 4,
+            scratch_shapes=[
+                pltpu.VMEM((4, rows, tokens, features), jnp.bfloat16),
+                pltpu.SemaphoreType.DMA((2, 4)),
+            ],
+        )(*packed)
     )
 
 

time: 68.1 us -> 61.6 us (0.905)
  local copies, waits for them, and re-layouts: 7.34 us -> 0 us
  Pallas kernels: 59.1 us -> 60.1 us
    unnamed x14 -> x0, local copies, waits for them, and re-layouts: 7.34 us -> none
    pallas_call x0 -> x1, Pallas kernels: none -> 2.42 us  [local(): pl.pallas_call(settle, out_shape=(out, out, out, out), in_specs=[anywhere...]
    pallas_call x1, Pallas kernels: 59.1 us -> 57.7 us  [local(): pl.pallas_call(functools.partial(kernel, peers), out_shape=(out, out, out...]
where the time goes in v2:
time: 61.6 us; the launch traced here: 61.4 us
  Pallas kernels  60.1 us (98%)
  between operations  1.29 us (2%)
    pallas_call x1, Pallas kernels, local(): pl.pallas_call(functools.partial(kernel, peers), out_shape=(out, out, out...  57.7 us
    pallas_call x1, Pallas kernels, local(): pl.pallas_call(settle, out_shape=(out, out, out, out), in_specs=[anywhere...  2.42 us

profile of v2, /device:TPU:0, one launch (start us, length us, event | category | flops | bytes accessed | tf_op | source)
XLA Modules:
  0.0 61.4 jit_solution(15142588609613588161)
XLA Ops:
  1.3 57.7 %shard_map.93 = (bf16[1,128,2048]{2,1,0:T(8,128)(2,1)}, bf16[1,128,2048]{2,1,0:T(8,128)(2,1)}, bf16[1,128,2048]{2,1,0:T(8,128)(2,1)}, bf16[1,128,2048]{2,1,0:T(8,128)(2,1)}) custom-call(s32[1,1,4]{2,1,0:T(1,128)} %neighbours_ref.1, s32[1,1]{1,0:T(1,128)S(6)} %copy.10.counts_ref, bf16[1,128,2048]{2,1,0:T(8,128)(2,1)} %q_ref.1, bf16[1,128,2048]{2,1,0:T(8,128)(2,1)} %k_ref.1, ...), custom_call_target="tpu_custom_call" | custom-call | flops 2500000000 | bytes 4194304 | tf_op jit(solution)/shard_map/pallas_call | solution.py:364
  59.0 2.4 %shard_map.94 = (bf16[1,128,2048]{2,1,0:T(8,128)(2,1)}, bf16[1,128,2048]{2,1,0:T(8,128)(2,1)}, bf16[1,128,2048]{2,1,0:T(8,128)(2,1)}, bf16[1,128,2048]{2,1,0:T(8,128)(2,1)}) custom-call(bf16[1,128,2048]{2,1,0:T(8,128)(2,1)} %get-tuple-element.8.refs_0_, bf16[1,128,2048]{2,1,0:T(8,128)(2,1)} %get-tuple-element.9.refs_1_, ...), custom_call_target="tpu_custom_call" | custom-call | tf_op jit(solution)/shard_map/pallas_call | solution.py:390

commit v3 on v1

--- a/solution.py
+++ b/solution.py
@@ -15,7 +15,8 @@
 HALF = HEADS // 2
 SLOTS = 6
 AHEAD = 2
-BEHIND = 1
+BEHIND = 2
+LATE = 4
 INV_ROOT = HEAD_DIM ** (-0.5)
 MESH = pl.DeviceIdType.MESH
 
@@ -30,10 +31,10 @@
 
 def kernel(
     peers,
-    neighbours_ref, counts_ref, q_ref, k_ref, v_ref, g_ref,
+    near_ref, count_ref, q_ref, k_ref, v_ref, g_ref,
     att_ref, gq_ref, gk_ref, gv_ref,
     kv, qg, share_out, share_in, result, own, bias,
-    send_sem, recv_sem, local_sem, bias_sem,
+    neighbours_ref, counts_ref, send_sem, recv_sem, local_sem, bias_sem, list_sem,
 ):
     me = lax.axis_index("mp")
     side = lax.rem(me, 2)
@@ -134,11 +135,20 @@
     def _():
         pl.semaphore_signal(barrier, inc=1, device_id={"mp": down}, device_id_type=MESH)
 
+    lists = (
+        pltpu.make_async_copy(near_ref, neighbours_ref, list_sem.at[0]),
+        pltpu.make_async_copy(count_ref, counts_ref, list_sem.at[1]),
+    )
+    for copy in lists:
+        copy.start()
+
     @pl.loop(0, HALF)
     def _(h):
         for i in range(4):
             keep(i, h).start()
 
+    for copy in lists:
+        copy.wait()
     tile = 2 * pair - 2 + lax.broadcasted_iota(jnp.int32, (8, TILE), 0)
     present = tile == me
     listed_count = counts_ref[0, 0]
@@ -315,45 +325,74 @@
         def _():
             finish(h - BEHIND)
 
-    for h in range(HALF - BEHIND, HALF):
-        finish(h)
-
-    bias_copy(side).wait_send()
-
-    @pl.loop(0, HALF)
-    def _(h):
+    def drain_inputs(h):
         for i in range(4):
             give(i, h).wait_send()
-            write(i, h).wait()
-            take_back(i, h).wait_recv()
-            hand_back(i, h).wait_send()
 
         @pl.when(has_up)
         def _():
             own_up(0, h).wait_send()
             own_up(1, h).wait_send()
             pass_up(h).wait_send()
-            share_up(h).wait_send()
 
         @pl.when(has_down)
         def _():
             own_down(0, h).wait_send()
             own_down(1, h).wait_send()
             pass_down(h).wait_send()
+
+    def drain_outputs(h):
+        for i in range(4):
+            write(i, h).wait()
+            hand_back(i, h).wait_send()
+            take_back(i, h).wait_recv()
+
+        @pl.when(has_up)
+        def _():
+            share_up(h).wait_send()
+
+        @pl.when(has_down)
+        def _():
             share_down(h).wait_send()
+
+    bias_copy(side).wait_send()
+
+    @pl.loop(0, HALF)
+    def _(h):
+        drain_inputs(h)
+
+    @pl.loop(0, HALF - LATE)
+    def _(h):
+        drain_outputs(h)
+
+    for h in range(HALF - BEHIND, HALF):
+        finish(h)
+
+    @pl.loop(HALF - LATE, HALF)
+    def _(h):
+        drain_outputs(h)
+
+
+def settle(a_ref, b_ref, c_ref, d_ref, p_ref, q_ref, r_ref, s_ref, sem):
+    pairs = zip((a_ref, b_ref, c_ref, d_ref), (p_ref, q_ref, r_ref, s_ref))
+    copies = [
+        pltpu.make_async_copy(src, dst, sem.at[i]) for i, (src, dst) in enumerate(pairs)
+    ]
+    for copy in copies:
+        copy.start()
+    for copy in copies:
+        copy.wait()
 
 
 def local(peers, queries, keys, values, grad_out, neighbours, counts):
     rows, tokens, features = queries.shape
     anywhere = pl.BlockSpec(memory_space=pl.ANY)
-    scalars = pl.BlockSpec(memory_space=pltpu.SMEM)
     out = jax.ShapeDtypeStruct((rows, tokens, features), jnp.bfloat16)
-    return tuple(
-        pl.pallas_call(
+    packed = pl.pallas_call(
             functools.partial(kernel, peers),
-            out_shape=(out, out, out, out),
-            in_specs=[scalars, scalars, anywhere, anywhere, anywhere, anywhere],
-            out_specs=(anywhere, anywhere, anywhere, anywhere),
+            out_shape=(pltpu.VMEM((rows, tokens, features), jnp.bfloat16),) * 4,
+            in_specs=[anywhere, anywhere, anywhere, anywhere, anywhere, anywhere],
+            out_specs=(pl.BlockSpec(memory_space=pltpu.VMEM),) * 4,
             scratch_shapes=[
                 pltpu.VMEM((HALF, 3, 2, 2, TILE, HEAD_DIM), jnp.bfloat16),
                 pltpu.VMEM((HALF, 2, 2, TILE, HEAD_DIM), jnp.bfloat16),
@@ -362,18 +401,30 @@
                 pltpu.VMEM((HALF, 2, 4, TILE, HEAD_DIM), jnp.bfloat16),
                 pltpu.VMEM((HALF, 2, 2, TILE, HEAD_DIM), jnp.float32),
                 pltpu.VMEM((2, 8, TILE), jnp.float32),
+                pltpu.SMEM(neighbours.shape, jnp.int32),
+                pltpu.SMEM(counts.shape, jnp.int32),
                 pltpu.SemaphoreType.DMA((HALF, 16)),
                 pltpu.SemaphoreType.DMA((HALF, 16)),
                 pltpu.SemaphoreType.DMA((HALF, 8)),
                 pltpu.SemaphoreType.DMA((2,)),
+                pltpu.SemaphoreType.DMA((2,)),
             ],
             compiler_params=pltpu.CompilerParams(
-                collective_id=0, has_side_effects=True, vmem_limit_bytes=40 * 1024 * 1024
+                collective_id=0, has_side_effects=True, vmem_limit_bytes=61 * 1024 * 1024
             ),
             cost_estimate=pl.CostEstimate(
                 flops=2_500_000_000, bytes_accessed=4_194_304, transcendentals=1_600_000
             ),
         )(neighbours, counts, queries, keys, values, grad_out)
+    return tuple(
+        pl.pallas_call(
+            settle,
+            out_shape=(out, out, out, out),
+            in_specs=[anywhere] * 4,
+            out_specs=(anywhere,) * 4,
+            scratch_shapes=[pltpu.SemaphoreType.DMA((4,))],
+            compiler_params=pltpu.CompilerParams(vmem_limit_bytes=2 * 1024 * 1024),
+        )(*packed)
     )
 
 

time: 68.1 us -> 59.7 us (0.88)
  local copies, waits for them, and re-layouts: 7.34 us -> 0 us
  Pallas kernels: 59.1 us -> 58.3 us
    unnamed x14 -> x0, local copies, waits for them, and re-layouts: 7.34 us -> none
    pallas_call x1 -> x2, Pallas kernels: 59.1 us -> 58.3 us  [the longest x1 56.9 us: local(): pl.pallas_call(functools.partial(kernel, peers), out_shape=(pltpu.VMEM((r...]
where the time goes in v3:
time: 59.7 us; the launch traced here: 59.6 us
  Pallas kernels  58.3 us (98%)
  between operations  1.29 us (2%)
    pallas_call x1, Pallas kernels, local(): pl.pallas_call(functools.partial(kernel, peers), out_shape=(pltpu.VMEM((r...  56.9 us
    pallas_call x1, Pallas kernels, local(): pl.pallas_call(settle, out_shape=(out, out, out, out), in_specs=[anywhere...  1.35 us

profile of v3, /device:TPU:0, one launch (start us, length us, event | category | flops | bytes accessed | tf_op | source)
XLA Modules:
  0.0 59.6 jit_solution(8526062836400874116)
XLA Ops:
  1.3 56.9 %shard_map.93 = (bf16[1,128,2048]{2,1,0:T(8,128)(2,1)S(1)}, bf16[1,128,2048]{2,1,0:T(8,128)(2,1)S(1)}, bf16[1,128,2048]{2,1,0:T(8,128)(2,1)S(1)}, bf16[1,128,2048]{2,1,0:T(8,128)(2,1)S(1)}) custom-call(s32[1,1,4]{2,1,0:T(1,128)} %near_ref.1, s32[1,1]{1,0:T(1,128)S(6)} %copy.10.count_ref, bf16[1,128,2048]{2,1,0:T(8,128)(2,1)} %q_ref.1, ...), custom_call_target="tpu_custom_call" | custom-call | flops 2500000000 | bytes 4194304 | tf_op jit(solution)/shard_map/pallas_call | solution.py:391
  58.2 1.3 %shard_map.94 = (bf16[1,128,2048]{2,1,0:T(8,128)(2,1)}, bf16[1,128,2048]{2,1,0:T(8,128)(2,1)}, bf16[1,128,2048]{2,1,0:T(8,128)(2,1)}, bf16[1,128,2048]{2,1,0:T(8,128)(2,1)}) custom-call(bf16[1,128,2048]{2,1,0:T(8,128)(2,1)S(1)} %get-tuple-element.8.a_ref, bf16[1,128,2048]{2,1,0:T(8,128)(2,1)S(1)} %get-tuple-element.9.b_ref, ...), custom_call_target="tpu_custom_call" | custom-call | tf_op jit(solution)/shard_map/pallas_call | solution.py:420

commit v4 on v3

--- a/solution.py
+++ b/solution.py
@@ -14,9 +14,9 @@
 MAXN = 4
 HALF = HEADS // 2
 SLOTS = 6
-AHEAD = 2
-BEHIND = 2
-LATE = 4
+AHEAD = 3
+BEHIND = 3
+LATE = 5
 INV_ROOT = HEAD_DIM ** (-0.5)
 MESH = pl.DeviceIdType.MESH
 

time: 59.7 us -> 59.7 us (level)
  no operation moved by 1% of the time
where the time goes in v4:
time: 59.7 us; the launch traced here: 59.6 us
  Pallas kernels  58.3 us (98%)
  between operations  1.29 us (2%)
    pallas_call x1, Pallas kernels, local(): pl.pallas_call(functools.partial(kernel, peers), out_shape=(pltpu.VMEM((r...  56.9 us
    pallas_call x1, Pallas kernels, local(): pl.pallas_call(settle, out_shape=(out, out, out, out), in_specs=[anywhere...  1.35 us

profile of v4, /device:TPU:0, one launch (start us, length us, event | category | flops | bytes accessed | tf_op | source)
XLA Modules:
  0.0 59.6 jit_solution(14382953693451315282)
XLA Ops:
  1.3 56.9 %shard_map.93 = (bf16[1,128,2048]{2,1,0:T(8,128)(2,1)S(1)}, bf16[1,128,2048]{2,1,0:T(8,128)(2,1)S(1)}, bf16[1,128,2048]{2,1,0:T(8,128)(2,1)S(1)}, bf16[1,128,2048]{2,1,0:T(8,128)(2,1)S(1)}) custom-call(s32[1,1,4]{2,1,0:T(1,128)} %near_ref.1, s32[1,1]{1,0:T(1,128)S(6)} %copy.10.count_ref, bf16[1,128,2048]{2,1,0:T(8,128)(2,1)} %q_ref.1, ...), custom_call_target="tpu_custom_call" | custom-call | flops 2500000000 | bytes 4194304 | tf_op jit(solution)/shard_map/pallas_call | solution.py:391
  58.2 1.3 %shard_map.94 = (bf16[1,128,2048]{2,1,0:T(8,128)(2,1)}, bf16[1,128,2048]{2,1,0:T(8,128)(2,1)}, bf16[1,128,2048]{2,1,0:T(8,128)(2,1)}, bf16[1,128,2048]{2,1,0:T(8,128)(2,1)}) custom-call(bf16[1,128,2048]{2,1,0:T(8,128)(2,1)S(1)} %get-tuple-element.8.a_ref, bf16[1,128,2048]{2,1,0:T(8,128)(2,1)S(1)} %get-tuple-element.9.b_ref, ...), custom_call_target="tpu_custom_call" | custom-call | tf_op jit(solution)/shard_map/pallas_call | solution.py:420
